TPU v7x, 32 devices: a whole 2x2x4 slice. The times are simulated.
32 devices in a mesh: vec: 4 (over y, x), amp: 8 (over z, core).
Axes of the slice: x: 2, y: 2, z: 4, core: 2. Of those that a mesh axis runs over, the one named last changes fastest.
Arguments:
- chol: bfloat16 [16, 1024, 8192], P(None, 'amp', 'vec'), may hold values from -2.5 to 2.5
- amplitudes: bfloat16 [16, 256, 1024], P(None, 'amp'), may hold values from -0.125 to 0.125
- task_list: int32 [16, 4], replicated, may hold values from 0 to 15
- counts: int32 [8], replicated, may hold values from 0 to 2, as said below
Outputs:
- residual: bfloat16 [16, 256, 1024], P('vec', 'amp')
Inputs may be any that keep to these rules, and one draw needn't show every extreme that they name: The counts sum to 8, and one of them equals 2.
All inputs are finite; a program needn't handle non-finite values.
Results may differ from a plain program's by a relative error of at most 0.0055.
Values may be sent and summed in bfloat16 or wider, within the bound.
No kernel may reach another device: no remote copies, remote signals or barrier semaphores. Data moves between devices by JAX's collectives and lax.ppermute only.
A program may use at most 128 MiB of HBM per device.

v0:
```python
import functools

import jax
import jax.numpy as jnp
import numpy as np
from jax import lax
from jax.experimental import pallas as pl
from jax.experimental.pallas import tpu as pltpu
from jax.sharding import PartitionSpec as P

VB = 32
PAIRS = VB * VB
CORES = 2
CHIPS = 4
LANES = 128
VMEM = 60 * 1024 * 1024


def plan_layout(tasks, tiles):
    fields = {}
    at = 0
    for name, size in (("order", tiles), ("local", tasks), ("spread", tasks), ("amp", tasks),
                       ("out", tasks), ("swap", tasks)):
        fields[name] = (at, size)
        at += size
    return fields, at


def popcount(bits):
    bits = bits - ((bits >> 1) & 0x55555555)
    bits = (bits & 0x33333333) + ((bits >> 2) & 0x33333333)
    bits = (bits + (bits >> 4)) & 0x0F0F0F0F
    return (bits + (bits >> 8) + (bits >> 16) + (bits >> 24)) & 0xFF


def plan_kernel(tasks, tiles, most, classes, task_ref, count_ref, plan_ref, size_ref, work):
    fields, _ = plan_layout(tasks, tiles)
    first = {name: place[0] for name, place in fields.items()}
    at = jnp.int32(0)
    for owner in range(count_ref.shape[0]):
        for entry in range(most):
            live = entry < count_ref[owner]

            @pl.when(live)
            def _():
                for column in range(4):
                    work[at * 4 + column] = task_ref[column, owner * most + entry]

            at = at + live.astype(jnp.int32)
    x = [work[task * 4] for task in range(tasks)]
    y = [work[task * 4 + 1] for task in range(tasks)]
    one = jnp.int32(1)
    codes = 1 << tasks
    code = lax.broadcasted_iota(jnp.int32, (codes // LANES, LANES), 0) * LANES + lax.broadcasted_iota(
        jnp.int32, (codes // LANES, LANES), 1
    )
    bits = jnp.zeros_like(code)
    used = jnp.int32(0)
    for task in range(tasks):
        bits = bits | jnp.where((code >> task) & 1 == 1, one << y[task], one << x[task])
        used = used | (one << y[task]) | (one << x[task])
    best = jnp.min(popcount(bits) * codes + code) & (codes - 1)
    cover = jnp.int32(0)
    for task in range(tasks):
        cover = cover | (one << jnp.where((best >> task) & 1 == 1, y[task], x[task]))
    place = jnp.int32(0)
    sizes = []
    for group in (cover, used & ~cover, ~used):
        for tile in range(tiles):
            member = (group >> tile) & 1 == 1

            @pl.when(member)
            def _():
                plan_ref[first["order"] + place] = jnp.int32(tile)
                work[4 * tasks + tile] = place

            place = place + member.astype(jnp.int32)
        sizes.append(place)
    fits = jnp.int32(len(classes) - 1)
    for at, (spread, listed) in sorted(enumerate(classes), key=lambda entry: -sum(entry[1])):
        fits = jnp.where((sizes[0] <= spread) & (sizes[1] <= listed), at, fits)
    size_ref[0] = fits
    for task in range(tasks):
        swap = (best >> task) & 1 == 0
        plan_ref[first["local"] + task] = work[4 * tasks + jnp.where(swap, y[task], x[task])]
        plan_ref[first["spread"] + task] = work[4 * tasks + jnp.where(swap, x[task], y[task])]
        plan_ref[first["amp"] + task] = work[task * 4 + 2]
        plan_ref[first["out"] + task] = work[task * 4 + 3]
        plan_ref[first["swap"] + task] = swap.astype(jnp.int32)


def make_plan(tasks, tiles, classes, task_list, counts):
    fields, length = plan_layout(tasks, tiles)
    most = task_list.shape[0] // counts.shape[0]
    smem = pl.BlockSpec(memory_space=pltpu.SMEM)
    plan, size = pl.pallas_call(
        functools.partial(plan_kernel, tasks, tiles, most, classes),
        out_shape=[jax.ShapeDtypeStruct((length,), jnp.int32), jax.ShapeDtypeStruct((1,), jnp.int32)],
        in_specs=[smem] * 2,
        out_specs=[smem] * 2,
        scratch_shapes=[pltpu.SMEM((4 * tasks + tiles,), jnp.int32)],
        name="plan",
    )(task_list.T, counts)
    return plan, {name: plan[at : at + held] for name, (at, held) in fields.items()}, size[0]


def collect_kernel(lists, plan, *refs):
    sources, refs = refs[: len(lists)], refs[len(lists) :]
    outs, refs = refs[: len(lists)], refs[len(lists) :]
    *held, sems = refs
    moves = []
    for (first, each), source, out, slot in zip(lists, sources, outs, held):
        begin = lax.axis_index("vec") * each + first
        moves += [(source.at[plan[begin + at]], slot.at[at], out.at[at]) for at in range(out.shape[0])]
    loads = [pltpu.make_async_copy(move[0], move[1], sems.at[0, at]) for at, move in enumerate(moves)]
    stores = [pltpu.make_async_copy(move[1], move[2], sems.at[1, at]) for at, move in enumerate(moves)]
    for load in loads:
        load.start()
    for load, store in zip(loads, stores):
        load.wait()
        store.start()
    for store in stores:
        store.wait()


def collect(plan, *wanted):
    shapes = [(count, *array.shape[1:]) for _, _, count, array in wanted]
    total = sum(shape[0] for shape in shapes)
    any_spec = pl.BlockSpec(memory_space=pl.ANY)
    return pl.pallas_call(
        functools.partial(collect_kernel, [want[:2] for want in wanted]),
        out_shape=[jax.ShapeDtypeStruct(shape, jnp.bfloat16) for shape in shapes],
        in_specs=[pl.BlockSpec(memory_space=pltpu.SMEM)] + [any_spec] * len(wanted),
        out_specs=[any_spec] * len(wanted),
        scratch_shapes=[pltpu.VMEM(shape, jnp.bfloat16) for shape in shapes]
        + [pltpu.SemaphoreType.DMA((2, total))],
        compiler_params=pltpu.CompilerParams(vmem_limit_bytes=VMEM),
        name="collect",
    )(plan, *[want[3] for want in wanted])


def swap_fours(blocks):
    group = lax.broadcasted_iota(jnp.int32, blocks[0].shape, 1) // VB
    for bit in (1, 2):
        right = (group & bit) != 0
        shift = bit * VB
        moved = list(blocks)
        for low in range(4):
            if low & bit:
                continue
            high = low | bit
            moved[low] = jnp.where(right, pltpu.roll(blocks[high], shift, 1), blocks[low])
            moved[high] = jnp.where(right, blocks[high], pltpu.roll(blocks[low], LANES - shift, 1))
        blocks = moved
    return blocks


ACROSS = (((1,), (1,)), ((), ()))
SOURCES = 10


def ladder_kernel(first, bits, plan, *refs):
    sources, refs = refs[:SOURCES], refs[SOURCES:]
    amp_own, amp_sib, *outs, rows, amps, products, integral, sems = refs
    own_a, own_b, sib_a, sib_b, fed_a, fed_b, sfed_a, sfed_b, mid_a, mid_b = sources
    pairs = ((own_a, own_b), (sib_a, sib_b), (fed_a, fed_b), (sfed_a, sfed_b))
    wide = (own_a, fed_a, mid_a, mid_b)
    slots, each_row, _ = own_a.shape
    each = amp_own.shape[2]
    step = pl.program_id(0)
    columns = amp_own.shape[0]
    column = lax.axis_index("vec")
    core = lax.rem(lax.axis_index("amp"), CORES)
    bit_of = lambda at: sum(jnp.where(at // each == which, bit, 0) for which, bit in enumerate(bits))
    task_of = lambda at: lax.rem(at, each) * columns + (bit_of(at) ^ column)
    part = lambda slot, side, block: rows.at[slot, side, pl.ds(block * each_row, each_row)]

    def amp_copies(task, slot):
        return [
            pltpu.make_async_copy(
                source.at[task // each, :, lax.rem(task, each)],
                amps.at[slot, :, holder],
                sems.at[slot, 2 * len(wide) + at],
            )
            for at, (source, holder) in enumerate(((amp_own, core), (amp_sib, 1 - core)))
        ]

    def start(task, slot):
        swap = plan[first["swap"] + task]
        at = plan[first["local"] + task]
        for block, (early, late) in enumerate(pairs):
            target, sem = part(slot, swap, block), sems.at[slot, block]

            @pl.when(at < slots)
            def _():
                pltpu.make_async_copy(early.at[at], target, sem).start()

            @pl.when(at >= slots)
            def _():
                pltpu.make_async_copy(late.at[at - slots], target, sem).start()

        at = plan[first["spread"] + task]
        for block, source in enumerate(wide):
            target, sem = part(slot, 1 - swap, block), sems.at[slot, len(wide) + block]
            pltpu.make_async_copy(source.at[at], target, sem).start()
        for copy in amp_copies(task, slot):
            copy.start()

    def wait(task, slot):
        swap = plan[first["swap"] + task]
        for block in range(len(wide)):
            for side, at in ((swap, block), (1 - swap, len(wide) + block)):
                pltpu.make_async_copy(own_a.at[0], part(slot, side, block), sems.at[slot, at]).wait()
        for copy in amp_copies(task, slot):
            copy.wait()

    @pl.when(step == 0)
    def _():
        start(task_of(0), 0)

    @pl.when(step + 1 < pl.num_programs(0))
    def _():
        start(task_of(step + 1), lax.rem(step + 1, 2))

    slot = lax.rem(step, 2)
    wait(task_of(step), slot)
    whole_products = lax.dot_general(
        rows[slot, 0], rows[slot, 1], ACROSS, preferred_element_type=jnp.float32
    )
    for block in range(products.shape[0]):
        products[block] = whole_products[:, block * LANES : (block + 1) * LANES]
    group = products.shape[1] // VB
    for high in range(VB // 4):
        for block in range(products.shape[0]):
            starts = [high * 4 + low for low in range(4)]
            blocks = [products[block, pl.ds(at, group, VB)].astype(jnp.bfloat16) for at in starts]
            for low, moved in enumerate(swap_fours(blocks)):
                to = (block * 4 + low) * group
                integral[to : to + group, high * LANES : (high + 1) * LANES] = moved
    upper = lax.axis_index("amp") >= CHIPS * CORES // 2
    order = [jnp.where(upper, CHIPS - 1 - chip, chip) for chip in range(CHIPS)]
    mine = jnp.concatenate([amps[slot, chip] for chip in order]).reshape(-1, amps.shape[-1])
    term = lax.dot_general(mine, integral[...], ACROSS, preferred_element_type=jnp.float32)
    for which, out in enumerate(outs):

        @pl.when(step // each == which)
        def _():
            out[0] = term.astype(jnp.bfloat16)


def ladder(first, bits, plan, blocks, amps):
    _, rows, depth = blocks[0].shape
    columns, chips, each, amp_rows, pairs = amps[0].shape
    occupied = chips * CORES * amp_rows
    side = 4 * rows
    terms = (side // VB) ** 2
    tasks = len(bits) * each

    def out_spec(which):
        half = lambda step: jnp.clip(step - which * each, 0, each - 1)
        return pl.BlockSpec((1, occupied, terms), lambda step, plan: (half(step), 0, 0))

    return pl.pallas_call(
        functools.partial(ladder_kernel, first, bits),
        out_shape=[jax.ShapeDtypeStruct((each, occupied, terms), jnp.bfloat16)] * len(bits),
        grid_spec=pltpu.PrefetchScalarGridSpec(
            num_scalar_prefetch=1,
            grid=(tasks,),
            in_specs=[pl.BlockSpec(memory_space=pl.ANY)] * (SOURCES + len(amps)),
            out_specs=[out_spec(which) for which in range(len(bits))],
            scratch_shapes=[
                pltpu.VMEM((2, 2, side, depth), jnp.bfloat16),
                pltpu.VMEM((2, chips, CORES, amp_rows, pairs), jnp.bfloat16),
                pltpu.VMEM((side // LANES, side, LANES), jnp.float32),
                pltpu.VMEM((terms, pairs), jnp.bfloat16),
                pltpu.SemaphoreType.DMA((2, 10)),
            ],
        ),
        compiler_params=pltpu.CompilerParams(vmem_limit_bytes=VMEM),
        cost_estimate=pl.CostEstimate(
            flops=tasks * 6 * (side * side * depth + occupied * terms * pairs),
            bytes_accessed=tasks * 2 * (2 * side * depth + occupied * pairs),
            transcendentals=0,
        ),
        name="ladder",
    )(plan, *blocks, *amps)


def routes():
    last = CHIPS - 1
    feed = [(0, 1), (last, last - 1)]
    middle = [(1, 2), (2, 1)]
    both = lambda hops: [(a * CORES + c, b * CORES + c) for a, b in hops for c in range(CORES)]
    sibling = [(a * CORES + c, a * CORES + 1 - c) for a in range(CHIPS) for c in range(CORES)]
    return both(feed), both(middle), sibling


def swap_columns(array, bit, columns):
    return lax.ppermute(array, "vec", perm=[(column, column ^ bit) for column in range(columns)])


def products(first, slots, listed, twice, chol, amplitudes, plan, each):
    feed, middle, sibling = routes()
    send = functools.partial(lax.ppermute, axis_name="amp")
    start = first["order"]
    (mine,) = collect(plan, (first["amp"], each, each, amplitudes))
    end = send(mine, perm=feed)
    (own_a,) = collect(plan, (start, 0, slots, chol))
    own_a, chol = lax.optimization_barrier((own_a, chol))
    mid_a = send(own_a, perm=middle)
    fed_a = send(own_a, perm=feed)
    (own_b,) = collect(plan, (start + slots, 0, listed - slots, chol))
    sib_a = send(own_a, perm=sibling)
    over = send(mine, perm=middle)
    far = send(end, perm=middle)
    line = jnp.stack([end, mine, over])
    own_b, fed_a, mid_a, sib_a, line, far = lax.optimization_barrier(
        (own_b, fed_a, mid_a, sib_a, line, far)
    )
    mid_b = send(fed_a, perm=middle)
    fed_b = send(own_b, perm=feed)
    sib_b = send(own_b, perm=sibling)
    sfed_a = send(fed_a, perm=sibling)
    amps = lax.all_gather(jnp.concatenate([line, far[None]]), "vec", axis=0, tiled=False)
    amps = (amps, send(amps, perm=sibling))
    fed_b, mid_b, sib_b, sfed_a, amps = lax.optimization_barrier((fed_b, mid_b, sib_b, sfed_a, amps))
    sfed_b = send(fed_b, perm=sibling)
    blocks = (own_a, own_b, sib_a, sib_b, fed_a, fed_b, sfed_a, sfed_b, mid_a, mid_b)
    columns = lax.axis_size("vec")
    away = list(range(columns))[:0:-1]
    arrived = []
    for call in ([away, [0]] if twice else [[*away, 0]]):
        for bit, term in zip(call, ladder(first, call, plan, blocks, amps)):
            arrived.append(swap_columns(term, bit, columns) if bit else term)
    return sum(term.astype(jnp.float32) for term in arrived).astype(jnp.bfloat16)


def target_columns(swap):
    worker, right, left = np.meshgrid(
        np.arange(2 * CORES), np.arange(VB // 2), np.arange(VB // 2), indexing="ij"
    )
    core = worker % CORES
    chip = 1 + worker // CORES
    near = np.where(chip == 1, 0, CHIPS - 1)
    far = np.where(chip == 1, 2, 1)
    end = np.where(chip == 1, CHIPS - 1, 0)
    each = VB // (CHIPS * CORES)

    def local(at):
        block = at // each
        home = np.where(block < 2, chip, near) * CORES + np.where(block % 2 == 0, core, 1 - core)
        return home * each + at % each

    def spread(at):
        return (np.choose(at // each, [chip, near, far, end]) * CORES + core) * each + at % each

    a, b = (spread(left), local(right)) if swap else (local(left), spread(right))
    return (a * VB + b).reshape(-1)


def scatter_terms(terms, named, tiles):
    columns = lax.axis_size("vec")
    column = lax.axis_index("vec")
    owners = lax.axis_size("amp")
    halves, rows, width = terms.shape
    each = rows // owners
    mine = terms.reshape(halves, owners, each, width).swapaxes(0, 1)
    mine = lax.all_to_all(mine, "amp", split_axis=0, concat_axis=0, tiled=True)
    mine = mine[CORES : CORES * (CHIPS - 1)].transpose(1, 2, 0, 3).reshape(halves * each, PAIRS)
    canonical = jnp.arange(PAIRS, dtype=jnp.int32)[None, :]
    one_hot = lambda to: (jnp.asarray(to, jnp.int32)[:, None] == canonical).astype(jnp.bfloat16)
    straight, turned = one_hot(target_columns(False)), one_hot(target_columns(True))
    dot = functools.partial(jnp.dot, preferred_element_type=jnp.float32)
    straight, turned = dot(mine, straight), dot(mine, turned)
    swap = named["swap"].reshape(halves, columns)
    out = named["out"].reshape(halves, columns)
    swapped = jnp.repeat(lax.dynamic_index_in_dim(swap, column, 1), each, axis=0) == 1
    placed = jnp.where(swapped, turned, straight).astype(jnp.bfloat16).reshape(halves, each, PAIRS)
    held = tiles // columns
    here = column * held + jnp.arange(held, dtype=jnp.int32)
    total = jnp.zeros((held, each, PAIRS), jnp.float32)
    for bit in range(columns):
        arrived = placed if bit == 0 else swap_columns(placed, bit, columns)
        targets = lax.dynamic_index_in_dim(out, column ^ bit, 1, keepdims=False)
        for half in range(halves):
            named_here = (here == targets[half])[:, None, None]
            total = total + jnp.where(named_here, arrived[half].astype(jnp.float32)[None], 0.0)
    return total.astype(jnp.bfloat16)


def line_local(chol, amplitudes, task_list, counts):
    tasks = lax.axis_size("amp")
    tiles = chol.shape[0]
    each = tasks // lax.axis_size("vec")
    half = tasks // 2
    classes = [(half + 1, tasks + 3), (half + 1, tasks + 2), (half, tasks + 1), (half + 2, tasks + 4)]
    classes.append((tasks, min(2 * tasks, tiles)))
    plan, named, branch = make_plan(tasks, tiles, classes, task_list, counts)
    first = {name: place[0] for name, place in plan_layout(tasks, tiles)[0].items()}
    def run(slots, listed):
        twice = slots < tasks
        return lambda: products(first, slots, listed, twice, chol, amplitudes, plan, each)

    terms = lax.switch(branch, [run(*sizes) for sizes in classes])
    return scatter_terms(terms, named, tiles)


def integral_tile(x_rows, y_rows):
    products = lax.dot_general(
        x_rows, y_rows, (((1,), (1,)), ((), ())), preferred_element_type=jnp.float32
    )
    return (
        products.reshape(VB, VB, VB, VB).transpose(0, 2, 1, 3).reshape(PAIRS, PAIRS).astype(jnp.bfloat16)
    )


def task_term(x_rows, y_rows, amp_rows):
    products = lax.dot_general(
        amp_rows, integral_tile(x_rows, y_rows), (((1,), (1,)), ((), ())), preferred_element_type=jnp.float32
    )
    return products.astype(jnp.bfloat16)


def spread_local(chol, amplitudes, task_list, counts):
    owners = lax.axis_size("amp")
    most = task_list.shape[0] // owners
    rank = jnp.arange(owners, dtype=jnp.int32)[:, None]
    offsets = jnp.cumsum(counts) - counts
    inside = (rank >= offsets) & (rank < offsets + counts)
    starts = jnp.arange(owners, dtype=jnp.int32) * most
    fields = task_list[jnp.sum(jnp.where(inside, starts + rank - offsets, 0), axis=1)]
    trade = functools.partial(lax.all_to_all, axis_name="amp", tiled=True)
    fetch = lambda array, which: trade(jnp.take(array, which, axis=0), split_axis=0, concat_axis=0).reshape(
        -1, array.shape[2]
    )
    term = task_term(fetch(chol, fields[:, 0]), fetch(chol, fields[:, 1]), fetch(amplitudes, fields[:, 2]))
    returned = trade(term.reshape(owners, -1, PAIRS), split_axis=0, concat_axis=0)
    tiles = amplitudes.shape[0]
    chosen = (jnp.arange(tiles, dtype=jnp.int32)[:, None] == fields[:, 3][None, :]).astype(jnp.bfloat16)
    summed = jnp.dot(chosen, returned.reshape(owners, -1), preferred_element_type=jnp.float32)
    summed = summed.reshape(tiles, -1, PAIRS)
    return lax.psum_scatter(summed, "vec", scatter_dimension=0, tiled=True).astype(jnp.bfloat16)


def solution(mesh):
    placed = (P(None, "amp", "vec"), P(None, "amp", None), P(), P())
    local = line_local if mesh.shape["amp"] == CHIPS * CORES else spread_local
    return jax.shard_map(
        local, mesh=mesh, in_specs=placed, out_specs=P("vec", "amp", None), check_vma=False
    )
```

profile of v0, /device:TPU:0, one launch (start us, length us, event | category | flops | bytes accessed | tf_op | source)
XLA Modules:
  0.0 219.7 jit_solution(12023778993829853200)
XLA Ops:
  6.5 1.8 plan.1
  9.0 176.5 %conditional.2 = (bf16[2,256,256]{2,1,0:T(8,128)(2,1)S(1)}) conditional(s32[]{:T(128)} %bitcast.27, (s32[56]{0:T(128)S(1)}, bf16[16,128,2048]{2,1,0:T(8,128)(2,1)}, bf16[16,32,1024]{2,1,0:T(8,128)(2,1)}) %tuple.41, (s32[56]{0:T(128)S(1)}, bf16[16,128,2048]{2,1,0:T(8,128)(2,1)}, ...), branch_computations={%region_0.0_spmd, %region_1.0_spmd, %region_2.0_spmd, %region_3.0_... | conditional | flops 28992733184 | bytes 209191616
  9.0 3.1 %collect.18.refs_0_ = bf16[5,128,2048]{2,1,0:T(8,128)(2,1)} custom-call(s32[56]{0:T(128)S(1)} %get-tuple-element.63.plan, bf16[16,128,2048]{2,1,0:T(8,128)(2,1)} %get-tuple-element.66.refs_0_), custom_call_target="tpu_custom_call" | custom-call | tf_op jit(solution)/shard_map/cond/branch_1_fun/collect/pallas_call | solution.py:130
  12.2 5.1 %collective-permute-start.15 = (bf16[5,128,2048]{2,1,0:T(8,128)(2,1)}, bf16[5,128,2048]{2,1,0:T(8,128)(2,1)S(1)}, u32[]{:S(2)}, u32[]{:S(2)}) collective-permute-start(bf16[5,128,2048]{2,1,0:T(8,128)(2,1)} %collect.18.refs_0_), channel_id=1, source_target_pairs={{0,2},{1,3},{6,4},{7,5},{8,10},{9,11},{14,12},{15,13},{16,18},{17,... | collective-permute-start | bytes 7864328 | tf_op jit(solution)/shard_map/cond/branch_1_fun/ppermute | solution.py:311
  17.3 2.2 collective-permute-start.16
  19.5 1.4 collect.20
  20.9 2.7 %collective-permute-start.18 = (bf16[2,32,1024]{2,1,0:T(8,128)(2,1)}, bf16[2,32,1024]{2,1,0:T(8,128)(2,1)S(1)}, u32[]{:S(2)}, u32[]{:S(2)}) collective-permute-start(bf16[2,32,1024]{2,1,0:T(8,128)(2,1)} %collect.20), channel_id=1, source_target_pairs={{0,2},{1,3},{6,4},{7,5},{8,10},{9,11},{14,12},{15,13},{16,18},{17,... | collective-permute-start | bytes 393224 | tf_op jit(solution)/shard_map/cond/branch_1_fun/ppermute | solution.py:307
  24.3 52.1 %collective-permute-done.18 = bf16[2,32,1024]{2,1,0:T(8,128)(2,1)S(1)} collective-permute-done((bf16[2,32,1024]{2,1,0:T(8,128)(2,1)}, bf16[2,32,1024]{2,1,0:T(8,128)(2,1)S(1)}, u32[]{:S(2)}, u32[]{:S(2)}) %collective-permute-start.18) | collective-permute-done | bytes 131104 | tf_op jit(solution)/shard_map/cond/branch_1_fun/ppermute | solution.py:307
  77.0 3.2 %collect.19.refs_1_ = bf16[5,128,2048]{2,1,0:T(8,128)(2,1)} custom-call(s32[56]{0:T(128)S(1)} %get-tuple-element.63.plan, bf16[16,128,2048]{2,1,0:T(8,128)(2,1)} %get-tuple-element.66.refs_0_), custom_call_target="tpu_custom_call" | custom-call | tf_op jit(solution)/shard_map/cond/branch_1_fun/collect/pallas_call | solution.py:130
  80.4 1.0 pad_maximum_fusion.2
  81.4 8.6 %collective-permute-start.21 = (bf16[5,128,2048]{2,1,0:T(8,128)(2,1)}, bf16[5,128,2048]{2,1,0:T(8,128)(2,1)}, u32[]{:S(2)}, u32[]{:S(2)}) collective-permute-start(bf16[5,128,2048]{2,1,0:T(8,128)(2,1)} %collect.19.refs_1_), channel_id=1, source_target_pairs={{0,2},{1,3},{6,4},{7,5},{8,10},{9,11},{14,12},{15,13},{16,18},{17,... | collective-permute-start | bytes 7864328 | tf_op jit(solution)/shard_map/cond/branch_1_fun/ppermute | solution.py:321
  90.0 2.2 %collective-permute-start.22 = (bf16[5,128,2048]{2,1,0:T(8,128)(2,1)S(1)}, bf16[5,128,2048]{2,1,0:T(8,128)(2,1)}, u32[]{:S(2)}, u32[]{:S(2)}) collective-permute-start(bf16[5,128,2048]{2,1,0:T(8,128)(2,1)S(1)} %collective-permute-done.15.refs_4_), channel_id=1, source_target_pairs={{2,4},{3,5},{4,2},{5,3},{10,12},{11,13},{12,10},{13,11},{18,20},{1... | collective-permute-start | bytes 7864328 | tf_op jit(solution)/shard_map/cond/branch_1_fun/ppermute | solution.py:320
  92.7 28.0 %all-gather.13.cloned.1.call-done = bf16[16,2,32,1024]{3,2,1,0:T(8,128)(2,1)} async-done(((bf16[4,2,32,1024]{3,2,1,0:T(8,128)(2,1)}), bf16[16,2,32,1024]{3,2,1,0:T(8,128)(2,1)}) %all-gather.13.cloned.1.call-update) | async-done | bytes 2097168 | tf_op jit(solution)/shard_map/cond/branch_1_fun/all_gather | solution.py:324
  120.8 23.1 %collective-permute-done.21.refs_5_ = bf16[5,128,2048]{2,1,0:T(8,128)(2,1)} collective-permute-done((bf16[5,128,2048]{2,1,0:T(8,128)(2,1)}, bf16[5,128,2048]{2,1,0:T(8,128)(2,1)}, u32[]{:S(2)}, u32[]{:S(2)}) %collective-permute-start.21) | collective-permute-done | bytes 2621472 | tf_op jit(solution)/shard_map/cond/branch_1_fun/ppermute | solution.py:321
  144.0 5.2 %collective-permute-done.26.refs_7_ = bf16[5,128,2048]{2,1,0:T(8,128)(2,1)} collective-permute-done((bf16[5,128,2048]{2,1,0:T(8,128)(2,1)}, bf16[5,128,2048]{2,1,0:T(8,128)(2,1)}, u32[]{:S(2)}, u32[]{:S(2)}) %collective-permute-start.26) | collective-permute-done | bytes 2621472 | tf_op jit(solution)/shard_map/cond/branch_1_fun/ppermute | solution.py:327
  149.2 18.8 %ladder.11 = (bf16[2,256,256]{2,1,0:T(8,128)(2,1)}, bf16[2,256,256]{2,1,0:T(8,128)(2,1)}, bf16[2,256,256]{2,1,0:T(8,128)(2,1)}) custom-call(s32[56]{0:T(128)S(1)} %get-tuple-element.63.plan, bf16[5,128,2048]{2,1,0:T(8,128)(2,1)} %collect.18.refs_0_, bf16[5,128,2048]{2,1,0:T(8,128)(2,1)} %collect.19.refs_1_, ...), custom_call_target="tpu_custom_call" | custom-call | flops 21743271936 | bytes 28311552 | tf_op jit(solution)/shard_map/cond/branch_1_fun/ladder/pallas_call | solution.py:263
  168.1 1.6 collective-permute-start.29
  169.6 1.5 collective-permute-start.28
  171.7 8.5 %ladder.12 = bf16[2,256,256]{2,1,0:T(8,128)(2,1)} custom-call(s32[56]{0:T(128)S(1)} %get-tuple-element.63.plan, bf16[5,128,2048]{2,1,0:T(8,128)(2,1)} %collect.18.refs_0_, bf16[5,128,2048]{2,1,0:T(8,128)(2,1)} %collect.19.refs_1_, bf16[5,128,2048]{2,1,0:T(8,128)(2,1)} %collective-permute-done.17.refs_2_, ...), custom_call_target="tpu_custom_call" | custom-call | flops 7247757312 | bytes 9437184 | tf_op jit(solution)/shard_map/cond/branch_1_fun/ladder/pallas_call | solution.py:263
  180.2 2.4 %collective-permute-done.28 = bf16[2,256,256]{2,1,0:T(8,128)(2,1)S(1)} collective-permute-done((bf16[2,256,256]{2,1,0:T(8,128)(2,1)}, bf16[2,256,256]{2,1,0:T(8,128)(2,1)S(1)}, u32[]{:S(2)}, u32[]{:S(2)}) %collective-permute-start.28) | collective-permute-done | bytes 262176 | tf_op jit(solution)/shard_map/cond/branch_1_fun/ppermute | solution.py:299
  182.7 1.2 collective-permute-done.27
  183.8 1.1 convert_add_fusion.1
  185.5 0.7 copy.9
  186.2 5.0 %all-to-all-start = ((bf16[8,2,32,256]{3,2,1,0:T(8,128)(2,1)}), bf16[8,2,32,256]{3,2,1,0:T(8,128)(2,1)S(1)}, u32[]{:S(2)}, u32[]{:S(2)}) async-start(bf16[8,2,32,256]{3,2,1,0:T(8,128)(2,1)} %copy.9), calls=%async_computation | async-start | bytes 524288 | tf_op jit(solution)/shard_map/all_to_all | solution.py:368
  197.9 3.1 %all-to-all-done = bf16[8,2,32,256]{3,2,1,0:T(8,128)(2,1)S(1)} async-done(((bf16[8,2,32,256]{3,2,1,0:T(8,128)(2,1)}), bf16[8,2,32,256]{3,2,1,0:T(8,128)(2,1)S(1)}, u32[]{:S(2)}, u32[]{:S(2)}) %all-to-all-start) | async-done | bytes 262176 | tf_op jit(solution)/shard_map/all_to_all | solution.py:368
  201.1 0.9 fusion
  202.1 1.0 fusion.5
  203.0 1.8 collective-permute-start.77
  205.5 1.1 collective-permute-start.75
  206.6 3.5 %collective-permute-done.77 = bf16[2,32,1024]{2,1,0:T(8,128)(2,1)S(1)} collective-permute-done((bf16[2,32,1024]{2,1,0:T(8,128)(2,1)S(1)}, bf16[2,32,1024]{2,1,0:T(8,128)(2,1)S(1)}, u32[]{:S(2)}, u32[]{:S(2)}) %collective-permute-start.77) | collective-permute-done | bytes 131104 | tf_op jit(solution)/shard_map/ppermute | solution.py:299
  210.1 1.5 collective-permute-done.76
  211.7 1.1 add_convert_fusion
  (57 shorter events, 10.1 us)
Async XLA Ops:
  9.0 192.2 %copy-start.18 = (s32[1024]{0:T(1024)S(1)}, s32[1024]{0:T(1024)}, u32[]{:S(2)}) copy-start(s32[1024]{0:T(1024)} %constant.41.clone) | copy-start | bytes 12292
  9.0 111.8 %all-gather.13.cloned.1.call-start = ((), (), s32[]{:S(2)}) async-start(), calls=%async_computation.2 | async-start | bytes 2621440 | tf_op jit(solution)/shard_map/cond/branch_1_fun/all_gather | solution.py:324
  9.0 10.4 %copy-start.1 = (bf16[16,32,1024]{2,1,0:T(8,128)(2,1)S(1)}, bf16[16,32,1024]{2,1,0:T(8,128)(2,1)}, u32[]{:S(2)}) copy-start(bf16[16,32,1024]{2,1,0:T(8,128)(2,1)} %get-tuple-element.67.refs_0_) | copy-start | bytes 3145732 | tf_op jit(solution)/shard_map/conditional
  12.2 68.1 %collective-permute-start.15 = (bf16[5,128,2048]{2,1,0:T(8,128)(2,1)}, bf16[5,128,2048]{2,1,0:T(8,128)(2,1)S(1)}, u32[]{:S(2)}, u32[]{:S(2)}) collective-permute-start(bf16[5,128,2048]{2,1,0:T(8,128)(2,1)} %collect.18.refs_0_), channel_id=1, source_target_pairs={{0,2},{1,3},{6,4},{7,5},{8,10},{9,11},{14,12},{15,13},{16,18},{17,... | collective-permute-start | bytes 7864328 | tf_op jit(solution)/shard_map/cond/branch_1_fun/ppermute | solution.py:311
  17.3 63.0 %collective-permute-start.16 = (bf16[5,128,2048]{2,1,0:T(8,128)(2,1)}, bf16[5,128,2048]{2,1,0:T(8,128)(2,1)}, u32[]{:S(2)}, u32[]{:S(2)}) collective-permute-start(bf16[5,128,2048]{2,1,0:T(8,128)(2,1)} %collect.18.refs_0_), channel_id=1, source_target_pairs={{2,4},{3,5},{4,2},{5,3},{10,12},{11,13},{12,10},{13,11},{18,20},{1... | collective-permute-start | bytes 7864328 | tf_op jit(solution)/shard_map/cond/branch_1_fun/ppermute | solution.py:310
  19.5 60.9 %collective-permute-start.17 = (bf16[5,128,2048]{2,1,0:T(8,128)(2,1)}, bf16[5,128,2048]{2,1,0:T(8,128)(2,1)}, u32[]{:S(2)}, u32[]{:S(2)}) collective-permute-start(bf16[5,128,2048]{2,1,0:T(8,128)(2,1)} %collect.18.refs_0_), channel_id=1, source_target_pairs={{0,1},{1,0},{2,3},{3,2},{4,5},{5,4},{6,7},{7,6},{8,9},{9,8},{10,11... | collective-permute-start | bytes 7864328 | tf_op jit(solution)/shard_map/cond/branch_1_fun/ppermute | solution.py:313
  20.9 59.4 %copy-start.12 = (bf16[2,32,1024]{2,1,0:T(8,128)(2,1)S(1)}, bf16[2,32,1024]{2,1,0:T(8,128)(2,1)}, u32[]{:S(2)}) copy-start(bf16[2,32,1024]{2,1,0:T(8,128)(2,1)} %collect.20) | copy-start | bytes 393220 | tf_op jit(solution)/shard_map/conditional
  20.9 55.5 %collective-permute-start.18 = (bf16[2,32,1024]{2,1,0:T(8,128)(2,1)}, bf16[2,32,1024]{2,1,0:T(8,128)(2,1)S(1)}, u32[]{:S(2)}, u32[]{:S(2)}) collective-permute-start(bf16[2,32,1024]{2,1,0:T(8,128)(2,1)} %collect.20), channel_id=1, source_target_pairs={{0,2},{1,3},{6,4},{7,5},{8,10},{9,11},{14,12},{15,13},{16,18},{17,... | collective-permute-start | bytes 393224 | tf_op jit(solution)/shard_map/cond/branch_1_fun/ppermute | solution.py:307
  23.6 56.6 %collective-permute-start.19 = (bf16[2,32,1024]{2,1,0:T(8,128)(2,1)}, bf16[2,32,1024]{2,1,0:T(8,128)(2,1)S(1)}, u32[]{:S(2)}, u32[]{:S(2)}) collective-permute-start(bf16[2,32,1024]{2,1,0:T(8,128)(2,1)} %collect.20), channel_id=1, source_target_pairs={{2,4},{3,5},{4,2},{5,3},{10,12},{11,13},{12,10},{13,11},{18,20},{1... | collective-permute-start | bytes 393224 | tf_op jit(solution)/shard_map/cond/branch_1_fun/ppermute | solution.py:314
  76.4 3.9 %collective-permute-start.20 = (bf16[2,32,1024]{2,1,0:T(8,128)(2,1)S(1)}, bf16[2,32,1024]{2,1,0:T(8,128)(2,1)S(1)}, u32[]{:S(2)}, u32[]{:S(2)}) collective-permute-start(bf16[2,32,1024]{2,1,0:T(8,128)(2,1)S(1)} %collective-permute-done.18), channel_id=1, source_target_pairs={{2,4},{3,5},{4,2},{5,3},{10,12},{11,13},{12,10},{13,11},{18,20},{1... | collective-permute-start | bytes 393224 | tf_op jit(solution)/shard_map/cond/branch_1_fun/ppermute | solution.py:315
  80.3 68.9 %copy-start.9 = (bf16[5,128,2048]{2,1,0:T(8,128)(2,1)}, bf16[5,128,2048]{2,1,0:T(8,128)(2,1)S(1)}, u32[]{:S(2)}) copy-start(bf16[5,128,2048]{2,1,0:T(8,128)(2,1)S(1)} %collective-permute-done.15.refs_4_) | copy-start | bytes 7864324 | tf_op jit(solution)/shard_map/conditional
  81.4 62.5 %collective-permute-start.21 = (bf16[5,128,2048]{2,1,0:T(8,128)(2,1)}, bf16[5,128,2048]{2,1,0:T(8,128)(2,1)}, u32[]{:S(2)}, u32[]{:S(2)}) collective-permute-start(bf16[5,128,2048]{2,1,0:T(8,128)(2,1)} %collect.19.refs_1_), channel_id=1, source_target_pairs={{0,2},{1,3},{6,4},{7,5},{8,10},{9,11},{14,12},{15,13},{16,18},{17,... | collective-permute-start | bytes 7864328 | tf_op jit(solution)/shard_map/cond/branch_1_fun/ppermute | solution.py:321
  90.0 53.8 %collective-permute-start.22 = (bf16[5,128,2048]{2,1,0:T(8,128)(2,1)S(1)}, bf16[5,128,2048]{2,1,0:T(8,128)(2,1)}, u32[]{:S(2)}, u32[]{:S(2)}) collective-permute-start(bf16[5,128,2048]{2,1,0:T(8,128)(2,1)S(1)} %collective-permute-done.15.refs_4_), channel_id=1, source_target_pairs={{2,4},{3,5},{4,2},{5,3},{10,12},{11,13},{12,10},{13,11},{18,20},{1... | collective-permute-start | bytes 7864328 | tf_op jit(solution)/shard_map/cond/branch_1_fun/ppermute | solution.py:320
  92.2 51.6 %collective-permute-start.23 = (bf16[5,128,2048]{2,1,0:T(8,128)(2,1)}, bf16[5,128,2048]{2,1,0:T(8,128)(2,1)}, u32[]{:S(2)}, u32[]{:S(2)}) collective-permute-start(bf16[5,128,2048]{2,1,0:T(8,128)(2,1)} %collect.19.refs_1_), channel_id=1, source_target_pairs={{0,1},{1,0},{2,3},{3,2},{4,5},{5,4},{6,7},{7,6},{8,9},{9,8},{10,11... | collective-permute-start | bytes 7864328 | tf_op jit(solution)/shard_map/cond/branch_1_fun/ppermute | solution.py:322
  92.2 51.6 %collective-permute-start.24 = (bf16[5,128,2048]{2,1,0:T(8,128)(2,1)S(1)}, bf16[5,128,2048]{2,1,0:T(8,128)(2,1)}, u32[]{:S(2)}, u32[]{:S(2)}) collective-permute-start(bf16[5,128,2048]{2,1,0:T(8,128)(2,1)S(1)} %collective-permute-done.15.refs_4_), channel_id=1, source_target_pairs={{0,1},{1,0},{2,3},{3,2},{4,5},{5,4},{6,7},{7,6},{8,9},{9,8},{10,11... | collective-permute-start | bytes 7864328 | tf_op jit(solution)/shard_map/cond/branch_1_fun/ppermute | solution.py:323
  120.8 23.1 %collective-permute-start.25 = (bf16[4,4,2,32,1024]{4,3,2,1,0:T(8,128)(2,1)}, bf16[4,4,2,32,1024]{4,3,2,1,0:T(8,128)(2,1)}, u32[]{:S(2)}, u32[]{:S(2)}) collective-permute-start(bf16[4,4,2,32,1024]{4,3,2,1,0:T(8,128)(2,1)} %bitcast.79), channel_id=1, source_target_pairs={{0,1},{1,0},{2,3},{3,2},{4,5},{5,4},{6,7},{7,6},{8,9},{9,8},{10,11... | collective-permute-start | bytes 6291464 | tf_op jit(solution)/shard_map/cond/branch_1_fun/ppermute | solution.py:325
  143.9 5.3 %collective-permute-start.26 = (bf16[5,128,2048]{2,1,0:T(8,128)(2,1)}, bf16[5,128,2048]{2,1,0:T(8,128)(2,1)}, u32[]{:S(2)}, u32[]{:S(2)}) collective-permute-start(bf16[5,128,2048]{2,1,0:T(8,128)(2,1)} %collective-permute-done.21.refs_5_), channel_id=1, source_target_pairs={{0,1},{1,0},{2,3},{3,2},{4,5},{5,4},{6,7},{7,6},{8,9},{9,8},{10,11... | collective-permute-start | bytes 7864328 | tf_op jit(solution)/shard_map/cond/branch_1_fun/ppermute | solution.py:327
  168.1 12.2 %collective-permute-start.29 = (bf16[2,256,256]{2,1,0:T(8,128)(2,1)}, bf16[2,256,256]{2,1,0:T(8,128)(2,1)S(1)}, u32[]{:S(2)}, u32[]{:S(2)}) collective-permute-start(bf16[2,256,256]{2,1,0:T(8,128)(2,1)} %get-tuple-element.82), channel_id=1, source_target_pairs={{0,8},{8,0},{16,24},{24,16},{1,9},{9,1},{17,25},{25,17},{2,10},{10... | collective-permute-start | bytes 786440 | tf_op jit(solution)/shard_map/cond/branch_1_fun/ppermute | solution.py:299
  169.6 13.0 %collective-permute-start.28 = (bf16[2,256,256]{2,1,0:T(8,128)(2,1)}, bf16[2,256,256]{2,1,0:T(8,128)(2,1)S(1)}, u32[]{:S(2)}, u32[]{:S(2)}) collective-permute-start(bf16[2,256,256]{2,1,0:T(8,128)(2,1)} %get-tuple-element.81), channel_id=1, source_target_pairs={{0,16},{8,24},{16,0},{24,8},{1,17},{9,25},{17,1},{25,9},{2,18},{10... | collective-permute-start | bytes 786440 | tf_op jit(solution)/shard_map/cond/branch_1_fun/ppermute | solution.py:299
  171.2 12.7 %collective-permute-start.27 = (bf16[2,256,256]{2,1,0:T(8,128)(2,1)}, bf16[2,256,256]{2,1,0:T(8,128)(2,1)S(1)}, u32[]{:S(2)}, u32[]{:S(2)}) collective-permute-start(bf16[2,256,256]{2,1,0:T(8,128)(2,1)} %get-tuple-element.80), channel_id=1, source_target_pairs={{0,24},{8,16},{16,8},{24,0},{1,25},{9,17},{17,9},{25,1},{2,26},{10... | collective-permute-start | bytes 786440 | tf_op jit(solution)/shard_map/cond/branch_1_fun/ppermute | solution.py:299
  185.4 16.6 %copy-start.17 = (s32[1024]{0:T(1024)S(1)}, s32[1024]{0:T(1024)}, u32[]{:S(2)}) copy-start(s32[1024]{0:T(1024)} %constant.40.clone) | copy-start | bytes 12292
  186.2 14.8 %all-to-all-start = ((bf16[8,2,32,256]{3,2,1,0:T(8,128)(2,1)}), bf16[8,2,32,256]{3,2,1,0:T(8,128)(2,1)S(1)}, u32[]{:S(2)}, u32[]{:S(2)}) async-start(bf16[8,2,32,256]{3,2,1,0:T(8,128)(2,1)} %copy.9), calls=%async_computation | async-start | bytes 524288 | tf_op jit(solution)/shard_map/all_to_all | solution.py:368
  203.0 7.1 %collective-permute-start.77 = (bf16[2,32,1024]{2,1,0:T(8,128)(2,1)S(1)}, bf16[2,32,1024]{2,1,0:T(8,128)(2,1)S(1)}, u32[]{:S(2)}, u32[]{:S(2)}) collective-permute-start(bf16[2,32,1024]{2,1,0:T(8,128)(2,1)S(1)} %bitcast.95), channel_id=1, source_target_pairs={{0,24},{8,16},{16,8},{24,0},{1,25},{9,17},{17,9},{25,1},{2,26},{10... | collective-permute-start | bytes 393224 | tf_op jit(solution)/shard_map/ppermute | solution.py:299
  204.8 6.8 %collective-permute-start.76 = (bf16[2,32,1024]{2,1,0:T(8,128)(2,1)S(1)}, bf16[2,32,1024]{2,1,0:T(8,128)(2,1)S(1)}, u32[]{:S(2)}, u32[]{:S(2)}) collective-permute-start(bf16[2,32,1024]{2,1,0:T(8,128)(2,1)S(1)} %bitcast.96), channel_id=1, source_target_pairs={{0,16},{8,24},{16,0},{24,8},{1,17},{9,25},{17,1},{25,9},{2,18},{10... | collective-permute-start | bytes 393224 | tf_op jit(solution)/shard_map/ppermute | solution.py:299
  205.5 6.2 %collective-permute-start.75 = (bf16[2,32,1024]{2,1,0:T(8,128)(2,1)S(1)}, bf16[2,32,1024]{2,1,0:T(8,128)(2,1)S(1)}, u32[]{:S(2)}, u32[]{:S(2)}) collective-permute-start(bf16[2,32,1024]{2,1,0:T(8,128)(2,1)S(1)} %bitcast.97), channel_id=1, source_target_pairs={{0,8},{8,0},{16,24},{24,16},{1,9},{9,1},{17,25},{25,17},{2,10},{10... | collective-permute-start | bytes 393224 | tf_op jit(solution)/shard_map/ppermute | solution.py:299
Sparse Core Ops, SparseCore 0:
  81.5 39.2 all-gather.12
where the time goes:
time: 220 us
  waiting for transfers between devices  120 us (55%)
  Pallas kernels  36.9 us (17%)
  starting transfers between devices  34.9 us (16%)
  between operations  14.2 us (6%)
  other arithmetic  8.32 us (4%)
  local copies, waits for them, and re-layouts  2.49 us (1%)
    ppermute x1, waiting for transfers between devices, products(): end = send(mine, perm=feed)  52.1 us
    all_gather x1, waiting for transfers between devices, products(): lax.all_gather(jnp.concatenate([line, far[None]]), 'vec', axis=0, tiled=F...  28 us
    pallas_call x2, Pallas kernels, ladder(): pl.pallas_call(functools.partial(ladder_kernel, first, bits), out_shape=[...  27.4 us
    ppermute x1, waiting for transfers between devices, products(): fed_b = send(own_b, perm=feed)  23.1 us
    ppermute x6, waiting for transfers between devices, swap_columns(): lax.ppermute(array, 'vec', perm=[(column, column ^ bit) for column in ran...  8.64 us
    ppermute x1, starting transfers between devices, products(): fed_b = send(own_b, perm=feed)  8.63 us
    pallas_call x3, Pallas kernels, collect(): pl.pallas_call(functools.partial(collect_kernel, [want[:2] for want in wa...  7.75 us
    ppermute x6, starting transfers between devices, swap_columns(): lax.ppermute(array, 'vec', perm=[(column, column ^ bit) for column in ran...  7.17 us
  transfers between devices with their start and end apart: 20, of which 9 were waited for; matrix products, arithmetic and copies ran while one was open for 3% of the time, Pallas kernels for 6%

commit v1 on v0

--- a/solution.py
+++ b/solution.py
@@ -312,6 +312,7 @@
     (own_b,) = collect(plan, (start + slots, 0, listed - slots, chol))
     sib_a = send(own_a, perm=sibling)
     over = send(mine, perm=middle)
+    end, own_b = lax.optimization_barrier((end, own_b))
     far = send(end, perm=middle)
     line = jnp.stack([end, mine, over])
     own_b, fed_a, mid_a, sib_a, line, far = lax.optimization_barrier(

time: 220 us -> 208 us (0.945)
  waiting for transfers between devices: 120 us -> 106 us
    ppermute x1, waiting for transfers between devices: 52.1 us -> 37.7 us  [products(): end = send(mine, perm=feed)]
where the time goes in v1:
time: 208 us; the launch traced here: 207 us
  waiting for transfers between devices  106 us (51%)
  Pallas kernels  36.8 us (18%)
  starting transfers between devices  36.3 us (17%)
  between operations  14.2 us (7%)
  other arithmetic  8.26 us (4%)
  local copies, waits for them, and re-layouts  3.06 us (1%)
    ppermute x1, waiting for transfers between devices, products(): end = send(mine, perm=feed)  37.7 us
    all_gather x1, waiting for transfers between devices, products(): lax.all_gather(jnp.concatenate([line, far[None]]), 'vec', axis=0, tiled=F...  29.4 us
    pallas_call x2, Pallas kernels, ladder(): pl.pallas_call(functools.partial(ladder_kernel, first, bits), out_shape=[...  27.4 us
    ppermute x1, waiting for transfers between devices, products(): fed_b = send(own_b, perm=feed)  22.3 us
    ppermute x1, starting transfers between devices, products(): fed_b = send(own_b, perm=feed)  10.5 us
    ppermute x6, waiting for transfers between devices, swap_columns(): lax.ppermute(array, 'vec', perm=[(column, column ^ bit) for column in ran...  8.47 us
    pallas_call x3, Pallas kernels, collect(): pl.pallas_call(functools.partial(collect_kernel, [want[:2] for want in wa...  7.57 us
    ppermute x6, starting transfers between devices, swap_columns(): lax.ppermute(array, 'vec', perm=[(column, column ^ bit) for column in ran...  7.1 us
  transfers between devices with their start and end apart: 20, of which 9 were waited for; matrix products, arithmetic and copies ran while one was open for 3% of the time, Pallas kernels for 6%

profile of v1, /device:TPU:0, one launch (start us, length us, event | category | flops | bytes accessed | tf_op | source)
XLA Modules:
  0.0 207.2 jit_solution(7214092361225797784)
XLA Ops:
  6.5 1.8 plan.1
  9.0 164.3 %conditional.2 = (bf16[2,256,256]{2,1,0:T(8,128)(2,1)S(1)}) conditional(s32[]{:T(128)} %bitcast.27, (s32[56]{0:T(128)S(1)}, bf16[16,128,2048]{2,1,0:T(8,128)(2,1)}, bf16[16,32,1024]{2,1,0:T(8,128)(2,1)}) %tuple.46, (s32[56]{0:T(128)S(1)}, bf16[16,128,2048]{2,1,0:T(8,128)(2,1)}, ...), branch_computations={%region_0.0_spmd, %region_1.0_spmd, %region_2.0_spmd, %region_3.0_... | conditional | flops 28992733184 | bytes 209191616
  9.3 3.0 %collect.21.refs_0_ = bf16[4,128,2048]{2,1,0:T(8,128)(2,1)} custom-call(s32[56]{0:T(128)S(1)} %get-tuple-element.87.plan, bf16[16,128,2048]{2,1,0:T(8,128)(2,1)} %get-tuple-element.91.refs_0_), custom_call_target="tpu_custom_call" | custom-call | tf_op jit(solution)/shard_map/cond/branch_2_fun/collect/pallas_call | solution.py:130
  12.3 5.1 %collective-permute-start.31 = (bf16[4,128,2048]{2,1,0:T(8,128)(2,1)}, bf16[4,128,2048]{2,1,0:T(8,128)(2,1)S(1)}, u32[]{:S(2)}, u32[]{:S(2)}) collective-permute-start(bf16[4,128,2048]{2,1,0:T(8,128)(2,1)} %collect.21.refs_0_), channel_id=1, source_target_pairs={{0,2},{1,3},{6,4},{7,5},{8,10},{9,11},{14,12},{15,13},{16,18},{17,... | collective-permute-start | bytes 6291464 | tf_op jit(solution)/shard_map/cond/branch_2_fun/ppermute | solution.py:311
  17.4 2.0 collective-permute-start.32
  19.3 1.4 collect.22
  20.8 2.9 %collective-permute-start.30 = (bf16[2,32,1024]{2,1,0:T(8,128)(2,1)}, bf16[2,32,1024]{2,1,0:T(8,128)(2,1)S(1)}, u32[]{:S(2)}, u32[]{:S(2)}) collective-permute-start(bf16[2,32,1024]{2,1,0:T(8,128)(2,1)} %collect.22), channel_id=1, source_target_pairs={{0,2},{1,3},{6,4},{7,5},{8,10},{9,11},{14,12},{15,13},{16,18},{17,... | collective-permute-start | bytes 393224 | tf_op jit(solution)/shard_map/cond/branch_2_fun/ppermute | solution.py:307
  24.4 3.1 %collect.23.refs_1_ = bf16[5,128,2048]{2,1,0:T(8,128)(2,1)} custom-call(s32[56]{0:T(128)S(1)} %get-tuple-element.87.plan, bf16[16,128,2048]{2,1,0:T(8,128)(2,1)} %get-tuple-element.91.refs_0_), custom_call_target="tpu_custom_call" | custom-call | tf_op jit(solution)/shard_map/cond/branch_2_fun/collect/pallas_call | solution.py:130
  27.5 37.7 %collective-permute-done.30 = bf16[2,32,1024]{2,1,0:T(8,128)(2,1)S(1)} collective-permute-done((bf16[2,32,1024]{2,1,0:T(8,128)(2,1)}, bf16[2,32,1024]{2,1,0:T(8,128)(2,1)S(1)}, u32[]{:S(2)}, u32[]{:S(2)}) %collective-permute-start.30) | collective-permute-done | bytes 131104 | tf_op jit(solution)/shard_map/cond/branch_2_fun/ppermute | solution.py:307
  66.0 0.9 pad_maximum_fusion.4
  67.5 10.5 %collective-permute-start.36 = (bf16[5,128,2048]{2,1,0:T(8,128)(2,1)}, bf16[5,128,2048]{2,1,0:T(8,128)(2,1)S(1)}, u32[]{:S(2)}, u32[]{:S(2)}) collective-permute-start(bf16[5,128,2048]{2,1,0:T(8,128)(2,1)} %collect.23.refs_1_), channel_id=1, source_target_pairs={{0,2},{1,3},{6,4},{7,5},{8,10},{9,11},{14,12},{15,13},{16,18},{17,... | collective-permute-start | bytes 7864328 | tf_op jit(solution)/shard_map/cond/branch_2_fun/ppermute | solution.py:322
  78.2 2.1 collective-permute-start.37
  80.7 29.4 %all-gather.15.cloned.1.call-done = bf16[16,2,32,1024]{3,2,1,0:T(8,128)(2,1)} async-done(((bf16[4,2,32,1024]{3,2,1,0:T(8,128)(2,1)}), bf16[16,2,32,1024]{3,2,1,0:T(8,128)(2,1)}) %all-gather.15.cloned.1.call-update) | async-done | bytes 2097168 | tf_op jit(solution)/shard_map/cond/branch_2_fun/all_gather | solution.py:325
  110.1 22.3 %collective-permute-done.36.refs_5_ = bf16[5,128,2048]{2,1,0:T(8,128)(2,1)S(1)} collective-permute-done((bf16[5,128,2048]{2,1,0:T(8,128)(2,1)}, bf16[5,128,2048]{2,1,0:T(8,128)(2,1)S(1)}, u32[]{:S(2)}, u32[]{:S(2)}) %collective-permute-start.36) | collective-permute-done | bytes 2621472 | tf_op jit(solution)/shard_map/cond/branch_2_fun/ppermute | solution.py:322
  132.5 5.0 %collective-permute-done.41.refs_7_ = bf16[5,128,2048]{2,1,0:T(8,128)(2,1)} collective-permute-done((bf16[5,128,2048]{2,1,0:T(8,128)(2,1)S(1)}, bf16[5,128,2048]{2,1,0:T(8,128)(2,1)}, u32[]{:S(2)}, u32[]{:S(2)}) %collective-permute-start.41) | collective-permute-done | bytes 2621472 | tf_op jit(solution)/shard_map/cond/branch_2_fun/ppermute | solution.py:328
  137.5 18.9 %ladder.13 = (bf16[2,256,256]{2,1,0:T(8,128)(2,1)}, bf16[2,256,256]{2,1,0:T(8,128)(2,1)}, bf16[2,256,256]{2,1,0:T(8,128)(2,1)}) custom-call(s32[56]{0:T(128)S(1)} %get-tuple-element.87.plan, bf16[4,128,2048]{2,1,0:T(8,128)(2,1)} %collect.21.refs_0_, bf16[5,128,2048]{2,1,0:T(8,128)(2,1)} %collect.23.refs_1_, ...), custom_call_target="tpu_custom_call" | custom-call | flops 21743271936 | bytes 28311552 | tf_op jit(solution)/shard_map/cond/branch_2_fun/ladder/pallas_call | solution.py:263
  156.4 1.6 collective-permute-start.44
  158.0 1.5 collective-permute-start.43
  160.0 8.6 %ladder.14 = bf16[2,256,256]{2,1,0:T(8,128)(2,1)} custom-call(s32[56]{0:T(128)S(1)} %get-tuple-element.87.plan, bf16[4,128,2048]{2,1,0:T(8,128)(2,1)} %collect.21.refs_0_, bf16[5,128,2048]{2,1,0:T(8,128)(2,1)} %collect.23.refs_1_, bf16[4,128,2048]{2,1,0:T(8,128)(2,1)} %collective-permute-done.33.refs_2_, ...), custom_call_target="tpu_custom_call" | custom-call | flops 7247757312 | bytes 9437184 | tf_op jit(solution)/shard_map/cond/branch_2_fun/ladder/pallas_call | solution.py:263
  168.5 3.3 %collective-permute-done.43 = bf16[2,256,256]{2,1,0:T(8,128)(2,1)S(1)} collective-permute-done((bf16[2,256,256]{2,1,0:T(8,128)(2,1)}, bf16[2,256,256]{2,1,0:T(8,128)(2,1)S(1)}, u32[]{:S(2)}, u32[]{:S(2)}) %collective-permute-start.43) | collective-permute-done | bytes 262176 | tf_op jit(solution)/shard_map/cond/branch_2_fun/ppermute | solution.py:299
  171.9 1.1 convert_add_fusion.2
  173.3 0.7 copy.9
  174.0 4.7 %all-to-all-start = ((bf16[8,2,32,256]{3,2,1,0:T(8,128)(2,1)}), bf16[8,2,32,256]{3,2,1,0:T(8,128)(2,1)S(1)}, u32[]{:S(2)}, u32[]{:S(2)}) async-start(bf16[8,2,32,256]{3,2,1,0:T(8,128)(2,1)} %copy.9), calls=%async_computation | async-start | bytes 524288 | tf_op jit(solution)/shard_map/all_to_all | solution.py:369
  185.3 3.1 %all-to-all-done = bf16[8,2,32,256]{3,2,1,0:T(8,128)(2,1)S(1)} async-done(((bf16[8,2,32,256]{3,2,1,0:T(8,128)(2,1)}), bf16[8,2,32,256]{3,2,1,0:T(8,128)(2,1)S(1)}, u32[]{:S(2)}, u32[]{:S(2)}) %all-to-all-start) | async-done | bytes 262176 | tf_op jit(solution)/shard_map/all_to_all | solution.py:369
  188.6 1.0 fusion
  189.5 1.0 fusion.5
  190.5 1.6 collective-permute-start.77
  192.1 1.2 collective-permute-start.76
  193.3 0.8 collective-permute-start.75
  194.1 3.7 %collective-permute-done.77 = bf16[2,32,1024]{2,1,0:T(8,128)(2,1)S(1)} collective-permute-done((bf16[2,32,1024]{2,1,0:T(8,128)(2,1)S(1)}, bf16[2,32,1024]{2,1,0:T(8,128)(2,1)S(1)}, u32[]{:S(2)}, u32[]{:S(2)}) %collective-permute-start.77) | collective-permute-done | bytes 131104 | tf_op jit(solution)/shard_map/ppermute | solution.py:299
  197.8 1.3 collective-permute-done.76
  199.3 1.1 add_convert_fusion
  (59 shorter events, 10.1 us)
Async XLA Ops:
  9.0 179.6 %copy-start.18 = (s32[1024]{0:T(1024)S(1)}, s32[1024]{0:T(1024)}, u32[]{:S(2)}) copy-start(s32[1024]{0:T(1024)} %constant.41.clone) | copy-start | bytes 12292
  9.2 100.9 %all-gather.15.cloned.1.call-start = ((), (), s32[]{:S(2)}) async-start(), calls=%async_computation.3 | async-start | bytes 2621440 | tf_op jit(solution)/shard_map/cond/branch_2_fun/all_gather | solution.py:325
  9.3 10.1 %copy-start.2 = (bf16[16,32,1024]{2,1,0:T(8,128)(2,1)S(1)}, bf16[16,32,1024]{2,1,0:T(8,128)(2,1)}, u32[]{:S(2)}) copy-start(bf16[16,32,1024]{2,1,0:T(8,128)(2,1)} %get-tuple-element.90.refs_0_) | copy-start | bytes 3145732 | tf_op jit(solution)/shard_map/conditional
  12.3 53.7 %collective-permute-start.31 = (bf16[4,128,2048]{2,1,0:T(8,128)(2,1)}, bf16[4,128,2048]{2,1,0:T(8,128)(2,1)S(1)}, u32[]{:S(2)}, u32[]{:S(2)}) collective-permute-start(bf16[4,128,2048]{2,1,0:T(8,128)(2,1)} %collect.21.refs_0_), channel_id=1, source_target_pairs={{0,2},{1,3},{6,4},{7,5},{8,10},{9,11},{14,12},{15,13},{16,18},{17,... | collective-permute-start | bytes 6291464 | tf_op jit(solution)/shard_map/cond/branch_2_fun/ppermute | solution.py:311
  17.4 48.6 %collective-permute-start.32 = (bf16[4,128,2048]{2,1,0:T(8,128)(2,1)}, bf16[4,128,2048]{2,1,0:T(8,128)(2,1)}, u32[]{:S(2)}, u32[]{:S(2)}) collective-permute-start(bf16[4,128,2048]{2,1,0:T(8,128)(2,1)} %collect.21.refs_0_), channel_id=1, source_target_pairs={{2,4},{3,5},{4,2},{5,3},{10,12},{11,13},{12,10},{13,11},{18,20},{1... | collective-permute-start | bytes 6291464 | tf_op jit(solution)/shard_map/cond/branch_2_fun/ppermute | solution.py:310
  19.3 46.7 %collective-permute-start.33 = (bf16[4,128,2048]{2,1,0:T(8,128)(2,1)}, bf16[4,128,2048]{2,1,0:T(8,128)(2,1)}, u32[]{:S(2)}, u32[]{:S(2)}) collective-permute-start(bf16[4,128,2048]{2,1,0:T(8,128)(2,1)} %collect.21.refs_0_), channel_id=1, source_target_pairs={{0,1},{1,0},{2,3},{3,2},{4,5},{5,4},{6,7},{7,6},{8,9},{9,8},{10,11... | collective-permute-start | bytes 6291464 | tf_op jit(solution)/shard_map/cond/branch_2_fun/ppermute | solution.py:313
  20.8 45.1 %copy-start.13 = (bf16[2,32,1024]{2,1,0:T(8,128)(2,1)S(1)}, bf16[2,32,1024]{2,1,0:T(8,128)(2,1)}, u32[]{:S(2)}) copy-start(bf16[2,32,1024]{2,1,0:T(8,128)(2,1)} %collect.22) | copy-start | bytes 393220 | tf_op jit(solution)/shard_map/conditional
  20.8 44.5 %collective-permute-start.30 = (bf16[2,32,1024]{2,1,0:T(8,128)(2,1)}, bf16[2,32,1024]{2,1,0:T(8,128)(2,1)S(1)}, u32[]{:S(2)}, u32[]{:S(2)}) collective-permute-start(bf16[2,32,1024]{2,1,0:T(8,128)(2,1)} %collect.22), channel_id=1, source_target_pairs={{0,2},{1,3},{6,4},{7,5},{8,10},{9,11},{14,12},{15,13},{16,18},{17,... | collective-permute-start | bytes 393224 | tf_op jit(solution)/shard_map/cond/branch_2_fun/ppermute | solution.py:307
  23.7 42.2 %collective-permute-start.34 = (bf16[2,32,1024]{2,1,0:T(8,128)(2,1)}, bf16[2,32,1024]{2,1,0:T(8,128)(2,1)S(1)}, u32[]{:S(2)}, u32[]{:S(2)}) collective-permute-start(bf16[2,32,1024]{2,1,0:T(8,128)(2,1)} %collect.22), channel_id=1, source_target_pairs={{2,4},{3,5},{4,2},{5,3},{10,12},{11,13},{12,10},{13,11},{18,20},{1... | collective-permute-start | bytes 393224 | tf_op jit(solution)/shard_map/cond/branch_2_fun/ppermute | solution.py:314
  65.2 0.7 collective-permute-start.35
  66.0 1.5 copy-start.10
  67.5 64.9 %collective-permute-start.36 = (bf16[5,128,2048]{2,1,0:T(8,128)(2,1)}, bf16[5,128,2048]{2,1,0:T(8,128)(2,1)S(1)}, u32[]{:S(2)}, u32[]{:S(2)}) collective-permute-start(bf16[5,128,2048]{2,1,0:T(8,128)(2,1)} %collect.23.refs_1_), channel_id=1, source_target_pairs={{0,2},{1,3},{6,4},{7,5},{8,10},{9,11},{14,12},{15,13},{16,18},{17,... | collective-permute-start | bytes 7864328 | tf_op jit(solution)/shard_map/cond/branch_2_fun/ppermute | solution.py:322
  78.1 54.3 %collective-permute-start.38 = (bf16[5,128,2048]{2,1,0:T(8,128)(2,1)}, bf16[5,128,2048]{2,1,0:T(8,128)(2,1)}, u32[]{:S(2)}, u32[]{:S(2)}) collective-permute-start(bf16[5,128,2048]{2,1,0:T(8,128)(2,1)} %collect.23.refs_1_), channel_id=1, source_target_pairs={{0,1},{1,0},{2,3},{3,2},{4,5},{5,4},{6,7},{7,6},{8,9},{9,8},{10,11... | collective-permute-start | bytes 7864328 | tf_op jit(solution)/shard_map/cond/branch_2_fun/ppermute | solution.py:323
  78.2 32.0 %collective-permute-start.37 = (bf16[4,128,2048]{2,1,0:T(8,128)(2,1)}, bf16[4,128,2048]{2,1,0:T(8,128)(2,1)}, u32[]{:S(2)}, u32[]{:S(2)}) collective-permute-start(bf16[4,128,2048]{2,1,0:T(8,128)(2,1)} %copy-done.10), channel_id=1, source_target_pairs={{2,4},{3,5},{4,2},{5,3},{10,12},{11,13},{12,10},{13,11},{18,20},{1... | collective-permute-start | bytes 6291464 | tf_op jit(solution)/shard_map/cond/branch_2_fun/ppermute | solution.py:321
  80.2 29.9 %collective-permute-start.39 = (bf16[4,128,2048]{2,1,0:T(8,128)(2,1)}, bf16[4,128,2048]{2,1,0:T(8,128)(2,1)}, u32[]{:S(2)}, u32[]{:S(2)}) collective-permute-start(bf16[4,128,2048]{2,1,0:T(8,128)(2,1)} %copy-done.10), channel_id=1, source_target_pairs={{0,1},{1,0},{2,3},{3,2},{4,5},{5,4},{6,7},{7,6},{8,9},{9,8},{10,11... | collective-permute-start | bytes 6291464 | tf_op jit(solution)/shard_map/cond/branch_2_fun/ppermute | solution.py:324
  110.1 22.3 %collective-permute-start.40 = (bf16[4,4,2,32,1024]{4,3,2,1,0:T(8,128)(2,1)}, bf16[4,4,2,32,1024]{4,3,2,1,0:T(8,128)(2,1)}, u32[]{:S(2)}, u32[]{:S(2)}) collective-permute-start(bf16[4,4,2,32,1024]{4,3,2,1,0:T(8,128)(2,1)} %bitcast.82), channel_id=1, source_target_pairs={{0,1},{1,0},{2,3},{3,2},{4,5},{5,4},{6,7},{7,6},{8,9},{9,8},{10,11... | collective-permute-start | bytes 6291464 | tf_op jit(solution)/shard_map/cond/branch_2_fun/ppermute | solution.py:326
  132.4 5.1 %copy-start.8 = (bf16[5,128,2048]{2,1,0:T(8,128)(2,1)}, bf16[5,128,2048]{2,1,0:T(8,128)(2,1)S(1)}, u32[]{:S(2)}) copy-start(bf16[5,128,2048]{2,1,0:T(8,128)(2,1)S(1)} %collective-permute-done.36.refs_5_) | copy-start | bytes 7864324 | tf_op jit(solution)/shard_map/conditional
  132.4 5.1 %collective-permute-start.41 = (bf16[5,128,2048]{2,1,0:T(8,128)(2,1)S(1)}, bf16[5,128,2048]{2,1,0:T(8,128)(2,1)}, u32[]{:S(2)}, u32[]{:S(2)}) collective-permute-start(bf16[5,128,2048]{2,1,0:T(8,128)(2,1)S(1)} %collective-permute-done.36.refs_5_), channel_id=1, source_target_pairs={{0,1},{1,0},{2,3},{3,2},{4,5},{5,4},{6,7},{7,6},{8,9},{9,8},{10,11... | collective-permute-start | bytes 7864328 | tf_op jit(solution)/shard_map/cond/branch_2_fun/ppermute | solution.py:328
  156.4 12.1 %collective-permute-start.44 = (bf16[2,256,256]{2,1,0:T(8,128)(2,1)}, bf16[2,256,256]{2,1,0:T(8,128)(2,1)S(1)}, u32[]{:S(2)}, u32[]{:S(2)}) collective-permute-start(bf16[2,256,256]{2,1,0:T(8,128)(2,1)} %get-tuple-element.108), channel_id=1, source_target_pairs={{0,8},{8,0},{16,24},{24,16},{1,9},{9,1},{17,25},{25,17},{2,10},{10... | collective-permute-start | bytes 786440 | tf_op jit(solution)/shard_map/cond/branch_2_fun/ppermute | solution.py:299
  158.0 13.9 %collective-permute-start.43 = (bf16[2,256,256]{2,1,0:T(8,128)(2,1)}, bf16[2,256,256]{2,1,0:T(8,128)(2,1)S(1)}, u32[]{:S(2)}, u32[]{:S(2)}) collective-permute-start(bf16[2,256,256]{2,1,0:T(8,128)(2,1)} %get-tuple-element.107), channel_id=1, source_target_pairs={{0,16},{8,24},{16,0},{24,8},{1,17},{9,25},{17,1},{25,9},{2,18},{10... | collective-permute-start | bytes 786440 | tf_op jit(solution)/shard_map/cond/branch_2_fun/ppermute | solution.py:299
  159.5 12.4 %collective-permute-start.42 = (bf16[2,256,256]{2,1,0:T(8,128)(2,1)}, bf16[2,256,256]{2,1,0:T(8,128)(2,1)S(1)}, u32[]{:S(2)}, u32[]{:S(2)}) collective-permute-start(bf16[2,256,256]{2,1,0:T(8,128)(2,1)} %get-tuple-element.106), channel_id=1, source_target_pairs={{0,24},{8,16},{16,8},{24,0},{1,25},{9,17},{17,9},{25,1},{2,26},{10... | collective-permute-start | bytes 786440 | tf_op jit(solution)/shard_map/cond/branch_2_fun/ppermute | solution.py:299
  173.3 16.3 %copy-start.17 = (s32[1024]{0:T(1024)S(1)}, s32[1024]{0:T(1024)}, u32[]{:S(2)}) copy-start(s32[1024]{0:T(1024)} %constant.40.clone) | copy-start | bytes 12292
  174.0 14.4 %all-to-all-start = ((bf16[8,2,32,256]{3,2,1,0:T(8,128)(2,1)}), bf16[8,2,32,256]{3,2,1,0:T(8,128)(2,1)S(1)}, u32[]{:S(2)}, u32[]{:S(2)}) async-start(bf16[8,2,32,256]{3,2,1,0:T(8,128)(2,1)} %copy.9), calls=%async_computation | async-start | bytes 524288 | tf_op jit(solution)/shard_map/all_to_all | solution.py:369
  190.5 7.3 %collective-permute-start.77 = (bf16[2,32,1024]{2,1,0:T(8,128)(2,1)S(1)}, bf16[2,32,1024]{2,1,0:T(8,128)(2,1)S(1)}, u32[]{:S(2)}, u32[]{:S(2)}) collective-permute-start(bf16[2,32,1024]{2,1,0:T(8,128)(2,1)S(1)} %bitcast.95), channel_id=1, source_target_pairs={{0,24},{8,16},{16,8},{24,0},{1,25},{9,17},{17,9},{25,1},{2,26},{10... | collective-permute-start | bytes 393224 | tf_op jit(solution)/shard_map/ppermute | solution.py:299
  192.1 7.1 %collective-permute-start.76 = (bf16[2,32,1024]{2,1,0:T(8,128)(2,1)S(1)}, bf16[2,32,1024]{2,1,0:T(8,128)(2,1)S(1)}, u32[]{:S(2)}, u32[]{:S(2)}) collective-permute-start(bf16[2,32,1024]{2,1,0:T(8,128)(2,1)S(1)} %bitcast.96), channel_id=1, source_target_pairs={{0,16},{8,24},{16,0},{24,8},{1,17},{9,25},{17,1},{25,9},{2,18},{10... | collective-permute-start | bytes 393224 | tf_op jit(solution)/shard_map/ppermute | solution.py:299
  193.3 6.0 %collective-permute-start.75 = (bf16[2,32,1024]{2,1,0:T(8,128)(2,1)S(1)}, bf16[2,32,1024]{2,1,0:T(8,128)(2,1)S(1)}, u32[]{:S(2)}, u32[]{:S(2)}) collective-permute-start(bf16[2,32,1024]{2,1,0:T(8,128)(2,1)S(1)} %bitcast.97), channel_id=1, source_target_pairs={{0,8},{8,0},{16,24},{24,16},{1,9},{9,1},{17,25},{25,17},{2,10},{10... | collective-permute-start | bytes 393224 | tf_op jit(solution)/shard_map/ppermute | solution.py:299
Sparse Core Ops, SparseCore 0:
  67.7 42.4 all-gather.14
